TPU v7x, 128 devices: a whole 4x4x4 slice. The times are simulated.
128 devices in a mesh: store: 8 (over x, core), sku: 16 (over z, y).
Axes of the slice: x: 4, y: 4, z: 4, core: 2. Of those that a mesh axis runs over, the one named last changes fastest.
Arguments:
- base_bottom: float32 [128, 13, 16384], P(('store', 'sku')), may hold values from -6 to 6
- weight_bottom: float32 [128, 13, 16384], P(('store', 'sku')), may hold values from 0.5 to 4
- base_category: float32 [128, 13, 1024], P(('store', 'sku')), may hold values from -24 to 24
- weight_category: float32 [128, 13, 1024], P(('store', 'sku')), may hold values from 0.02 to 0.2
- base_region: float32 [32, 13, 16384], P(None, None, ('store', 'sku')), may hold values from -24 to 24
- weight_region: float32 [32, 13, 16384], P(None, None, ('store', 'sku')), may hold values from 0.02 to 0.2
- category_map: int32 [16384], replicated, may hold values from 0 to 1023
- region_map: int32 [128], replicated, may hold values from 0 to 31
Outputs:
- reconciled: float32 [128, 13, 16384], P(('store', 'sku'))
- residual: float32 [128, 13, 16384], P(('store', 'sku'))
All inputs are finite; a program needn't handle non-finite values.
Results may differ from a plain program's by a relative error of at most 0.0003.
Values sent between devices are 32-bit elements; how exact they have to be, the bound alone decides.
A program may use at most 128 MiB of HBM per device.

v0:
```python
import math
import jax
import jax.numpy as jnp
from jax import lax
from jax.sharding import PartitionSpec as P

ITERS = 3


def table_times(table, values):
    return jnp.dot(
        table, values, precision=lax.Precision.HIGHEST, preferred_element_type=jnp.float32
    )


def category_sums(field, category_map, n_cat):
    stores, horizon, skus = field.shape
    rows = stores * horizon
    flat = field.reshape(rows, skus)
    width = math.gcd(skus, 2048)
    labels = jnp.arange(n_cat, dtype=jnp.int32)

    def accumulate(blocknum, total):
        start = blocknum * width
        columns = lax.dynamic_slice_in_dim(flat, start, width, 1)
        members = lax.dynamic_slice_in_dim(category_map, start, width, 0)
        onehot = (members[:, None] == labels[None, :]).astype(jnp.float32)
        return total + jnp.dot(
            columns, onehot, precision=lax.Precision.HIGHEST, preferred_element_type=jnp.float32
        )

    total = lax.fori_loop(0, skus // width, accumulate, jnp.zeros((rows, n_cat), jnp.float32))
    return total.reshape(stores, horizon, n_cat)


def category_spread(values, category_map, skus):
    stores, horizon, n_cat = values.shape
    rows = stores * horizon
    flat = values.reshape(rows, n_cat)
    width = math.gcd(skus, 2048)
    labels = jnp.arange(n_cat, dtype=jnp.int32)

    def place(blocknum, output):
        start = blocknum * width
        members = lax.dynamic_slice_in_dim(category_map, start, width, 0)
        onehot = (labels[:, None] == members[None, :]).astype(jnp.float32)
        block = jnp.dot(
            flat, onehot, precision=lax.Precision.HIGHEST, preferred_element_type=jnp.float32
        )
        return lax.dynamic_update_slice_in_dim(output, block, start, 1)

    output = lax.fori_loop(0, skus // width, place, jnp.zeros((rows, skus), jnp.float32))
    return output.reshape(stores, horizon, skus)


def to_region(field):
    return lax.all_to_all(field, ("store", "sku"), split_axis=2, concat_axis=0, tiled=True)


def from_region(field):
    return lax.all_to_all(field, ("store", "sku"), split_axis=0, concat_axis=2, tiled=True)


def squares(residual):
    return lax.psum(jnp.sum(residual * residual), ("store", "sku"))


def on_device(
    base_bottom,
    weight_bottom,
    base_category,
    weight_category,
    base_region,
    weight_region,
    category_map,
    region_map,
):
    n_cat = weight_category.shape[2]
    n_regions, horizon, sku_local = weight_region.shape
    skus = base_bottom.shape[2]
    all_stores = region_map.shape[0]
    region_ids = jnp.arange(n_regions, dtype=jnp.int32)
    gather_table = (region_ids[:, None] == region_map[None, :]).astype(jnp.float32)
    spread_table = (region_map[:, None] == region_ids[None, :]).astype(jnp.float32)

    def region_sums(field):
        moved = to_region(field).reshape(all_stores, horizon * sku_local)
        summed = table_times(gather_table, moved)
        return summed.reshape(n_regions, horizon, sku_local)

    def spread_both(cat_values, region_values):
        flat = region_values.reshape(n_regions, horizon * sku_local)
        spread = table_times(spread_table, flat)
        returned = from_region(spread.reshape(all_stores, horizon, sku_local))
        return category_spread(cat_values, category_map, skus) + returned

    reconciled = base_bottom
    region_start = weight_region * (base_region - region_sums(base_bottom))
    cat_start = weight_category * (base_category - category_sums(base_bottom, category_map, n_cat))
    residual = spread_both(cat_start, region_start)
    direction = residual
    norm_now = squares(residual)
    for repeat in range(ITERS):
        operate_region_values = weight_region * region_sums(direction)
        operate_cat_values = weight_category * category_sums(direction, category_map, n_cat)
        image = weight_bottom * direction + spread_both(operate_cat_values, operate_region_values)
        step_size = norm_now / lax.psum(jnp.sum(direction * image), ("store", "sku"))
        reconciled = reconciled + step_size * direction
        residual = residual - step_size * image
        norm_next = squares(residual)
        direction = residual + norm_next / norm_now * direction
        norm_now = norm_next
    return (reconciled, residual)


def solution(mesh):
    in_specs = (
        P(("store", "sku"), None, None),
        P(("store", "sku"), None, None),
        P(("store", "sku"), None, None),
        P(("store", "sku"), None, None),
        P(None, None, ("store", "sku")),
        P(None, None, ("store", "sku")),
        P(),
        P(),
    )
    out_specs = (P(("store", "sku"), None, None), P(("store", "sku"), None, None))
    return jax.shard_map(
        on_device, mesh=mesh, in_specs=in_specs, out_specs=out_specs, check_vma=False
    )
```

profile of v0, /device:TPU:1, one launch (start us, length us, event | category | flops | bytes accessed | tf_op | source)
XLA Modules:
  0.0 1191.2 jit_solution(167319318847375889)
XLA Ops:
  0.6 15.4 %copy.158 = f32[1,13,16384]{1,0,2:T(1,128)} copy(f32[1,13,16384]{2,0,1:T(1,128)} %param.24) | data formatting | bytes 1703936 | tf_op args[0]
  16.6 74.5 %reduce.2 = f32[16384,13]{1,0:T(8,128)} reduce(f32[16384,1,13]{2,1,0:T(1,128)} %bitcast.248, f32[]{:T(128)} %broadcast.52), dimensions={1}, to_apply=%bitcast.187.reduce_sub_computation | reduce | bytes 1703940
  112.5 22.1 %while.116 = (s32[]{:T(128)}, f32[13,1024]{1,0:T(8,128)S(1)}, f32[13,16384]{1,0:T(8,128)S(1)}, s32[16384]{0:T(1024)S(1)}, s32[]{:T(128)}, /*index=5*/s32[]{:T(128)}, s32[]{:T(128)}, s32[]{:T(128)}) while((s32[]{:T(128)}, f32[13,1024]{1,0:T(8,128)S(1)}, f32[13,16384]{1,0:T(8,128)S(1)}, s32[16384]{0:T(1024)S(1)}, s32[]{:T(128)}, ...), condition=%wide.region_1.0_spmd.clone, body=%wide.region_0.0_spmd.clone.sunk | while | flops 329279488 | bytes 274581 | solution.py:32
  152.0 15.1 %copy.159 = f32[1,13,16384]{2,0,1:T(1,128)S(1)} copy(f32[1,13,16384]{1,0,2:T(1,128)} %bitcast.249) | data formatting | bytes 1703936 | tf_op jit(solution)/shard_map/all_to_all | solution.py:57
  180.4 21.7 %while.112 = (s32[]{:T(128)}, f32[13,16384]{1,0:T(8,128)S(1)}, s32[16384]{0:T(1024)S(1)}, f32[13,1024]{1,0:T(8,128)S(1)}, s32[]{:T(128)}, /*index=5*/s32[]{:T(128)}, s32[]{:T(128)}, s32[]{:T(128)}) while((s32[]{:T(128)}, f32[13,16384]{1,0:T(8,128)S(1)}, s32[16384]{0:T(1024)S(1)}, f32[13,1024]{1,0:T(8,128)S(1)}, s32[]{:T(128)}, ...), condition=%wide.region_3.0_spmd.clone, body=%wide.region_2.0_spmd.clone.sunk | while | flops 329252864 | bytes 221323 | solution.py:52
  216.2 74.5 %reduce.4 = f32[16384,13]{1,0:T(8,128)} reduce(f32[16384,1,13]{2,1,0:T(1,128)} %bitcast.245, f32[]{:T(128)} %broadcast.52), dimensions={1}, to_apply=%bitcast.189.reduce_sub_computation | reduce | bytes 1703940
  309.7 22.1 %while.117 = (s32[]{:T(128)}, f32[13,1024]{1,0:T(8,128)S(1)}, f32[13,16384]{1,0:T(8,128)S(1)}, s32[16384]{0:T(1024)S(1)}, s32[]{:T(128)}, /*index=5*/s32[]{:T(128)}, s32[]{:T(128)}, s32[]{:T(128)}) while((s32[]{:T(128)}, f32[13,1024]{1,0:T(8,128)S(1)}, f32[13,16384]{1,0:T(8,128)S(1)}, s32[16384]{0:T(1024)S(1)}, s32[]{:T(128)}, ...), condition=%wide.region_7.0_spmd.clone, body=%wide.region_6.0_spmd.clone.sunk | while | flops 329279488 | bytes 274581 | solution.py:32
  377.9 21.7 %while.113 = (s32[]{:T(128)}, f32[13,16384]{1,0:T(8,128)S(1)}, s32[16384]{0:T(1024)S(1)}, f32[13,1024]{1,0:T(8,128)S(1)}, s32[]{:T(128)}, /*index=5*/s32[]{:T(128)}, s32[]{:T(128)}, s32[]{:T(128)}) while((s32[]{:T(128)}, f32[13,16384]{1,0:T(8,128)S(1)}, s32[16384]{0:T(1024)S(1)}, f32[13,1024]{1,0:T(8,128)S(1)}, s32[]{:T(128)}, ...), condition=%wide.region_9.0_spmd.clone, body=%wide.region_8.0_spmd.clone.sunk | while | flops 329252864 | bytes 221323 | solution.py:52
  404.7 67.3 %all-reduce = (f32[]{:T(128)}, f32[]{:T(128)}) all-reduce(f32[]{:T(128)} %get-tuple-element.960, f32[]{:T(128)} %multiply_reduce_fusion.4), channel_id=1, replica_groups=mesh['store'=8,'sku'=16] {'store','sku'}, use_global_device_ids=true, to_apply=%region_5.0 | all-reduce | flops 2 | bytes 16 | tf_op jit(solution)/shard_map/psum | solution.py:65
  476.8 62.9 %psum.44 = f32[]{:T(128)} all-reduce(f32[]{:T(128)} %get-tuple-element.958), channel_id=1, replica_groups=mesh['store'=8,'sku'=16] {'store','sku'}, use_global_device_ids=true, to_apply=%region_13.0 | all-reduce | flops 1 | bytes 8 | tf_op jit(solution)/shard_map/psum | solution.py:65
  554.5 74.6 %reduce.6 = f32[16384,13]{1,0:T(8,128)} reduce(f32[16384,1,13]{2,1,0:T(1,128)} %bitcast.246, f32[]{:T(128)} %broadcast.52), dimensions={1}, to_apply=%bitcast.191.reduce_sub_computation | reduce | bytes 1703940
  644.6 22.1 %while.118 = (s32[]{:T(128)}, f32[13,1024]{1,0:T(8,128)S(1)}, f32[13,16384]{1,0:T(8,128)S(1)}, s32[16384]{0:T(1024)S(1)}, s32[]{:T(128)}, /*index=5*/s32[]{:T(128)}, s32[]{:T(128)}, s32[]{:T(128)}) while((s32[]{:T(128)}, f32[13,1024]{1,0:T(8,128)S(1)}, f32[13,16384]{1,0:T(8,128)S(1)}, s32[16384]{0:T(1024)S(1)}, s32[]{:T(128)}, ...), condition=%wide.region_15.0_spmd.clone, body=%wide.region_14.0_spmd.clone.sunk | while | flops 329279488 | bytes 274581 | solution.py:32
  671.6 15.5 %reshape.143 = f32[16384,1,13]{2,1,0:T(1,128)} reshape(f32[128,1664]{1,0:T(8,128)} %reduce.7) | data formatting | bytes 1703936
  687.1 16.3 %copy.178 = f32[1,13,16384]{2,0,1:T(1,128)} copy(f32[1,13,16384]{1,0,2:T(1,128)} %bitcast.251) | data formatting | bytes 1703936 | tf_op jit(solution)/shard_map/all_to_all | solution.py:57
  721.2 26.8 %while.114 = (s32[]{:T(128)}, f32[13,16384]{1,0:T(8,128)}, s32[16384]{0:T(1024)S(1)}, f32[13,1024]{1,0:T(8,128)S(1)}, s32[]{:T(128)}, /*index=5*/s32[]{:T(128)}, s32[]{:T(128)}, s32[]{:T(128)}) while((s32[]{:T(128)}, f32[13,16384]{1,0:T(8,128)}, s32[16384]{0:T(1024)S(1)}, f32[13,1024]{1,0:T(8,128)S(1)}, s32[]{:T(128)}, ...), condition=%wide.region_17.0_spmd.clone, body=%wide.region_16.0_spmd.clone.sunk | while | flops 329252864 | bytes 209035 | solution.py:52
  753.6 67.2 %psum.45 = f32[]{:T(128)} all-reduce(f32[]{:T(128)} %multiply_reduce_fusion.2), channel_id=1, replica_groups=mesh['store'=8,'sku'=16] {'store','sku'}, use_global_device_ids=true, to_apply=%region_19.0 | all-reduce | flops 1 | bytes 8 | tf_op jit(solution)/shard_map/psum | solution.py:107
  826.2 62.9 %psum.46 = f32[]{:T(128)} all-reduce(f32[]{:T(128)} %get-tuple-element.956), channel_id=1, replica_groups=mesh['store'=8,'sku'=16] {'store','sku'}, use_global_device_ids=true, to_apply=%region_21.0 | all-reduce | flops 1 | bytes 8 | tf_op jit(solution)/shard_map/psum | solution.py:65
  892.8 15.6 %copy.186 = f32[1,13,16384]{1,0,2:T(1,128)} copy(f32[1,13,16384]{2,1,0:T(8,128)} %multiply_add_fusion) | data formatting | bytes 1703936 | tf_op jit(solution)/shard_map/add | solution.py:111
  908.4 74.6 %reduce.8 = f32[16384,13]{1,0:T(8,128)} reduce(f32[16384,1,13]{2,1,0:T(1,128)} %bitcast.247, f32[]{:T(128)} %broadcast.52), dimensions={1}, to_apply=%bitcast.193.reduce_sub_computation | reduce | bytes 1703940
  998.2 29.3 %while.119 = (s32[]{:T(128)}, f32[13,1024]{1,0:T(8,128)S(1)}, f32[13,16384]{1,0:T(8,128)}, s32[16384]{0:T(1024)S(1)}, s32[]{:T(128)}, /*index=5*/s32[]{:T(128)}, s32[]{:T(128)}, s32[]{:T(128)}) while((s32[]{:T(128)}, f32[13,1024]{1,0:T(8,128)S(1)}, f32[13,16384]{1,0:T(8,128)}, s32[16384]{0:T(1024)S(1)}, s32[]{:T(128)}, ...), condition=%wide.region_23.0_spmd.clone, body=%wide.region_22.0_spmd.clone.sunk | while | flops 329279488 | bytes 262293 | solution.py:32
  1032.4 15.5 %reshape.145 = f32[16384,1,13]{2,1,0:T(1,128)} reshape(f32[128,1664]{1,0:T(8,128)} %reduce.9) | data formatting | bytes 1703936
  1047.9 16.3 %copy.187 = f32[1,13,16384]{2,0,1:T(1,128)} copy(f32[1,13,16384]{1,0,2:T(1,128)} %bitcast.252) | data formatting | bytes 1703936 | tf_op jit(solution)/shard_map/all_to_all | solution.py:57
  1082.1 26.8 %while.115 = (s32[]{:T(128)}, f32[13,16384]{1,0:T(8,128)}, s32[16384]{0:T(1024)S(1)}, f32[13,1024]{1,0:T(8,128)S(1)}, s32[]{:T(128)}, /*index=5*/s32[]{:T(128)}, s32[]{:T(128)}, s32[]{:T(128)}) while((s32[]{:T(128)}, f32[13,16384]{1,0:T(8,128)}, s32[16384]{0:T(1024)S(1)}, f32[13,1024]{1,0:T(8,128)S(1)}, s32[]{:T(128)}, ...), condition=%wide.region_25.0_spmd.clone, body=%wide.region_24.0_spmd.clone.sunk | while | flops 329252864 | bytes 209035 | solution.py:52
  1114.9 67.2 %psum.47 = f32[]{:T(128)} all-reduce(f32[]{:T(128)} %multiply_reduce_fusion), channel_id=1, replica_groups=mesh['store'=8,'sku'=16] {'store','sku'}, use_global_device_ids=true, to_apply=%region_27.0 | all-reduce | flops 1 | bytes 8 | tf_op jit(solution)/shard_map/psum | solution.py:107
  (232 shorter events, 447.2 us)
Async XLA Ops:
  91.1 20.8 %copy-start.4 = (f32[1,13,16384]{2,0,1:T(1,128)S(1)}, f32[1,13,16384]{2,0,1:T(1,128)}, u32[]{:S(2)}) copy-start(f32[1,13,16384]{2,0,1:T(1,128)} %param.24) | copy-start | bytes 2555908
  91.1 21.3 %copy-start.6 = (s32[16384]{0:T(1024)S(1)}, s32[16384]{0:T(1024)}, u32[]{:S(2)}) copy-start(s32[16384]{0:T(1024)} %param.30) | copy-start | bytes 196612
  100.1 34.5 %copy-start.7 = (f32[1,13,1024]{2,0,1:T(1,128)S(1)}, f32[1,13,1024]{2,0,1:T(1,128)}, u32[]{:S(2)}) copy-start(f32[1,13,1024]{2,0,1:T(1,128)} %param.27) | copy-start | bytes 159748
  100.1 34.5 %copy-start.9 = (f32[1,13,1024]{2,0,1:T(1,128)S(1)}, f32[1,13,1024]{2,0,1:T(1,128)}, u32[]{:S(2)}) copy-start(f32[1,13,1024]{2,0,1:T(1,128)} %param.26) | copy-start | bytes 159748
  100.1 34.5 %all-to-all-start = ((f32[128,1,1664]{2,1,0:T(1,128)}), f32[128,1,1664]{2,1,0:T(1,128)S(1)}, u32[]{:S(2)}, u32[]{:S(2)}) async-start(f32[128,1,1664]{2,1,0:T(1,128)} %reshape.138), calls=%async_computation | async-start | bytes 1703936 | tf_op jit(solution)/shard_map/all_to_all | solution.py:57
  137.4 30.0 %copy-start.5 = (f32[32,13,128]{2,0,1:T(8,128)S(1)}, f32[32,13,128]{2,0,1:T(8,128)}, u32[]{:S(2)}) copy-start(f32[32,13,128]{2,0,1:T(8,128)} %param.29) | copy-start | bytes 638980
  137.4 30.0 %copy-start.8 = (f32[32,13,128]{2,0,1:T(8,128)S(1)}, f32[32,13,128]{2,0,1:T(8,128)}, u32[]{:S(2)}) copy-start(f32[32,13,128]{2,0,1:T(8,128)} %param.28) | copy-start | bytes 638980
  137.4 30.0 %copy-start.10 = (s32[128]{0:T(128)S(1)}, s32[128]{0:T(128)}, u32[]{:S(2)}) copy-start(s32[128]{0:T(128)} %param.31) | copy-start | bytes 1540
  170.1 32.1 %all-to-all-start.1 = ((f32[128,13,128]{2,1,0:T(8,128)}), f32[128,13,128]{2,1,0:T(8,128)S(1)}, u32[]{:S(2)}, u32[]{:S(2)}) async-start(f32[128,13,128]{2,1,0:T(8,128)} %copy.163), calls=%async_computation.1 | async-start | bytes 2097152 | tf_op jit(solution)/shard_map/all_to_all | solution.py:61
  299.7 32.2 %all-to-all-start.2 = ((f32[128,1,1664]{2,1,0:T(1,128)}), f32[128,1,1664]{2,1,0:T(1,128)S(1)}, u32[]{:S(2)}, u32[]{:S(2)}) async-start(f32[128,1,1664]{2,1,0:T(1,128)} %reshape.140), calls=%async_computation.2 | async-start | bytes 1703936 | tf_op jit(solution)/shard_map/all_to_all | solution.py:57
  367.2 32.5 %all-to-all-start.3 = ((f32[128,13,128]{2,1,0:T(8,128)}), f32[128,13,128]{2,1,0:T(8,128)}, u32[]{:S(2)}, u32[]{:S(2)}) async-start(f32[128,13,128]{2,1,0:T(8,128)} %copy.172), calls=%async_computation.3 | async-start | bytes 2097152 | tf_op jit(solution)/shard_map/all_to_all | solution.py:61
  377.9 24.4 %copy-start = (f32[1,13,16384]{2,0,1:T(1,128)S(1)}, f32[1,13,16384]{2,0,1:T(1,128)}, u32[]{:S(2)}) copy-start(f32[1,13,16384]{2,0,1:T(1,128)} %param.25) | copy-start | bytes 2555908
  399.7 2.0 copy-start.2
  638.1 28.7 %all-to-all-start.4 = ((f32[128,1,1664]{2,1,0:T(1,128)}), f32[128,1,1664]{2,1,0:T(1,128)}, u32[]{:S(2)}, u32[]{:S(2)}) async-start(f32[128,1,1664]{2,1,0:T(1,128)} %reshape.142), calls=%async_computation.4 | async-start | bytes 1703936 | tf_op jit(solution)/shard_map/all_to_all | solution.py:57
  709.5 38.4 %all-to-all-start.5 = ((f32[128,13,128]{2,1,0:T(8,128)}), f32[128,13,128]{2,1,0:T(8,128)}, u32[]{:S(2)}, u32[]{:S(2)}) async-start(f32[128,13,128]{2,1,0:T(8,128)} %copy.182), calls=%async_computation.5 | async-start | bytes 2097152 | tf_op jit(solution)/shard_map/all_to_all | solution.py:61
  750.2 1.0 copy-start.1
  991.9 35.7 %all-to-all-start.6 = ((f32[128,1,1664]{2,1,0:T(1,128)}), f32[128,1,1664]{2,1,0:T(1,128)}, u32[]{:S(2)}, u32[]{:S(2)}) async-start(f32[128,1,1664]{2,1,0:T(1,128)} %reshape.144), calls=%async_computation.6 | async-start | bytes 1703936 | tf_op jit(solution)/shard_map/all_to_all | solution.py:57
  1070.3 38.6 %all-to-all-start.7 = ((f32[128,13,128]{2,1,0:T(8,128)}), f32[128,13,128]{2,1,0:T(8,128)}, u32[]{:S(2)}, u32[]{:S(2)}) async-start(f32[128,13,128]{2,1,0:T(8,128)} %copy.191), calls=%async_computation.7 | async-start | bytes 2097152 | tf_op jit(solution)/shard_map/all_to_all | solution.py:61
  1111.1 1.0 copy-start.3
where the time goes:
time: 1200 us; the launch traced here: 1190 us
  other arithmetic  337 us (28%)
  blocking collectives  327 us (27%)
  local copies, waits for them, and re-layouts  242 us (20%)
  matrix products  199 us (17%)
  starting transfers between devices  77 us (6%)
    unnamed x8, other arithmetic  298 us
    psum x3, blocking collectives, squares(): return lax.psum(jnp.sum(residual * residual), ('store', 'sku'))  193 us
    psum x2, blocking collectives, on_device(): lax.psum(jnp.sum(direction * image), ('store', 'sku'))  134 us
    unnamed x43, local copies, waits for them, and re-layouts  121 us
    dot_general x32, matrix products, place(): jnp.dot(flat, onehot, precision=lax.Precision.HIGHEST, preferred_element_...  96.7 us
    dot_general x32, matrix products, accumulate(): jnp.dot(columns, onehot, precision=lax.Precision.HIGHEST, preferred_eleme...  95.5 us
    all_to_all x8, local copies, waits for them, and re-layouts, to_region(): lax.all_to_all(field, ('store', 'sku'), split_axis=2, concat_axis=0, tile...  68.1 us
    all_to_all x4, starting transfers between devices, from_region(): lax.all_to_all(field, ('store', 'sku'), split_axis=0, concat_axis=2, tile...  42.2 us
  transfers between devices with their start and end apart: 8, of which 0 were waited for; matrix products, arithmetic and copies ran while one was open for 16% of the time, Pallas kernels for 0%

commit v1 on v0

--- a/solution.py
+++ b/solution.py
@@ -58,7 +58,16 @@
 
 
 def from_region(field):
-    return lax.all_to_all(field, ("store", "sku"), split_axis=0, concat_axis=2, tiled=True)
+    meet_samples = lambda w_in, lane_axis: jnp.concatenate(
+        lax.all_to_all(
+            jnp.stack(jnp.split(w_in, lax.axis_size(lane_axis), 0), axis=0),
+            axis_name=lane_axis,
+            split_axis=0,
+            concat_axis=0,
+        ),
+        2,
+    )
+    return meet_samples(field, ("store", "sku"))
 
 
 def squares(residual):

time: 1200 us -> 1220 us (1.017)
  local copies, waits for them, and re-layouts: 242 us -> 255 us
    unnamed x43 -> x551, local copies, waits for them, and re-layouts: 121 us -> 122 us
where the time goes in v1:
time: 1220 us; the launch traced here: 1200 us
  other arithmetic  336 us (28%)
  blocking collectives  328 us (27%)
  local copies, waits for them, and re-layouts  255 us (21%)
  matrix products  199 us (16%)
  starting transfers between devices  75.2 us (6%)
    unnamed x8, other arithmetic  298 us
    psum x3, blocking collectives, squares(): return lax.psum(jnp.sum(residual * residual), ('store', 'sku'))  193 us
    psum x2, blocking collectives, on_device(): lax.psum(jnp.sum(direction * image), ('store', 'sku'))  135 us
    unnamed x551, local copies, waits for them, and re-layouts  122 us
    dot_general x32, matrix products, place(): jnp.dot(flat, onehot, precision=lax.Precision.HIGHEST, preferred_element_...  96.8 us
    dot_general x32, matrix products, accumulate(): jnp.dot(columns, onehot, precision=lax.Precision.HIGHEST, preferred_eleme...  95.5 us
    all_to_all x8, local copies, waits for them, and re-layouts, to_region(): lax.all_to_all(field, ('store', 'sku'), split_axis=2, concat_axis=0, tile...  69.7 us
    all_to_all x4, starting transfers between devices, from_region(): lax.all_to_all(jnp.stack(jnp.split(w_in, lax.axis_size(lane_axis), 0), ax...  40.5 us
  transfers between devices with their start and end apart: 8, of which 0 were waited for; matrix products, arithmetic and copies ran while one was open for 16% of the time, Pallas kernels for 0%

profile of v1, /device:TPU:1, one launch (start us, length us, event | category | flops | bytes accessed | tf_op | source)
XLA Modules:
  0.0 1204.9 jit_solution(11165120549861597428)
XLA Ops:
  16.5 74.4 %reduce.1026 = f32[16384,13]{1,0:T(8,128)} reduce(f32[16384,1,13]{2,1,0:T(1,128)} %bitcast.1222, f32[]{:T(128)} %broadcast.564), dimensions={1}, to_apply=%bitcast.1177.reduce_sub_computation | reduce | bytes 1703940
  112.4 22.1 %while.116 = (s32[]{:T(128)}, f32[13,1024]{1,0:T(8,128)S(1)}, f32[13,16384]{1,0:T(8,128)S(1)}, s32[16384]{0:T(1024)S(1)}, s32[]{:T(128)}, /*index=5*/s32[]{:T(128)}, s32[]{:T(128)}, s32[]{:T(128)}) while((s32[]{:T(128)}, f32[13,1024]{1,0:T(8,128)S(1)}, f32[13,16384]{1,0:T(8,128)S(1)}, s32[16384]{0:T(1024)S(1)}, s32[]{:T(128)}, ...), condition=%wide.region_1.0_spmd.clone, body=%wide.region_0.0_spmd.clone.sunk | while | flops 329279488 | bytes 274581 | solution.py:32
  151.9 15.7 %copy.214 = f32[1,13,16384]{2,0,1:T(1,128)S(1)} copy(f32[1,13,16384]{1,0,2:T(1,128)} %bitcast.1223) | data formatting | bytes 1703936 | tf_op jit(solution)/shard_map/all_to_all | solution.py:57
  184.7 21.7 %while.112 = (s32[]{:T(128)}, f32[13,16384]{1,0:T(8,128)S(1)}, s32[16384]{0:T(1024)S(1)}, f32[13,1024]{1,0:T(8,128)S(1)}, s32[]{:T(128)}, /*index=5*/s32[]{:T(128)}, s32[]{:T(128)}, s32[]{:T(128)}) while((s32[]{:T(128)}, f32[13,16384]{1,0:T(8,128)S(1)}, s32[16384]{0:T(1024)S(1)}, f32[13,1024]{1,0:T(8,128)S(1)}, s32[]{:T(128)}, ...), condition=%wide.region_3.0_spmd.clone, body=%wide.region_2.0_spmd.clone.sunk | while | flops 329252864 | bytes 221323 | solution.py:52
  220.2 74.4 %reduce.1028 = f32[16384,13]{1,0:T(8,128)} reduce(f32[16384,1,13]{2,1,0:T(1,128)} %bitcast.1219, f32[]{:T(128)} %broadcast.564), dimensions={1}, to_apply=%bitcast.1179.reduce_sub_computation | reduce | bytes 1703940
  313.7 22.1 %while.117 = (s32[]{:T(128)}, f32[13,1024]{1,0:T(8,128)S(1)}, f32[13,16384]{1,0:T(8,128)S(1)}, s32[16384]{0:T(1024)S(1)}, s32[]{:T(128)}, /*index=5*/s32[]{:T(128)}, s32[]{:T(128)}, s32[]{:T(128)}) while((s32[]{:T(128)}, f32[13,1024]{1,0:T(8,128)S(1)}, f32[13,16384]{1,0:T(8,128)S(1)}, s32[16384]{0:T(1024)S(1)}, s32[]{:T(128)}, ...), condition=%wide.region_7.0_spmd.clone, body=%wide.region_6.0_spmd.clone.sunk | while | flops 329279488 | bytes 274581 | solution.py:32
  353.0 15.5 %copy.222 = f32[1,13,16384]{2,0,1:T(1,128)S(1)} copy(f32[1,13,16384]{1,0,2:T(1,128)} %bitcast.1224) | data formatting | bytes 1703936 | tf_op jit(solution)/shard_map/all_to_all | solution.py:57
  385.7 21.7 %while.113 = (s32[]{:T(128)}, f32[13,16384]{1,0:T(8,128)S(1)}, s32[16384]{0:T(1024)S(1)}, f32[13,1024]{1,0:T(8,128)S(1)}, s32[]{:T(128)}, /*index=5*/s32[]{:T(128)}, s32[]{:T(128)}, s32[]{:T(128)}) while((s32[]{:T(128)}, f32[13,16384]{1,0:T(8,128)S(1)}, s32[16384]{0:T(1024)S(1)}, f32[13,1024]{1,0:T(8,128)S(1)}, s32[]{:T(128)}, ...), condition=%wide.region_9.0_spmd.clone, body=%wide.region_8.0_spmd.clone.sunk | while | flops 329252864 | bytes 221323 | solution.py:52
  412.2 67.4 %all-reduce = (f32[]{:T(128)}, f32[]{:T(128)}) all-reduce(f32[]{:T(128)} %get-tuple-element.1466, f32[]{:T(128)} %multiply_reduce_fusion.4), channel_id=1, replica_groups=mesh['store'=8,'sku'=16] {'store','sku'}, use_global_device_ids=true, to_apply=%region_5.0 | all-reduce | flops 2 | bytes 16 | tf_op jit(solution)/shard_map/psum | solution.py:74
  484.5 62.6 %psum.44 = f32[]{:T(128)} all-reduce(f32[]{:T(128)} %get-tuple-element.1464), channel_id=1, replica_groups=mesh['store'=8,'sku'=16] {'store','sku'}, use_global_device_ids=true, to_apply=%region_13.0 | all-reduce | flops 1 | bytes 8 | tf_op jit(solution)/shard_map/psum | solution.py:74
  561.8 74.4 %reduce.1030 = f32[16384,13]{1,0:T(8,128)} reduce(f32[16384,1,13]{2,1,0:T(1,128)} %bitcast.1220, f32[]{:T(128)} %broadcast.564), dimensions={1}, to_apply=%bitcast.1181.reduce_sub_computation | reduce | bytes 1703940
  651.5 22.1 %while.118 = (s32[]{:T(128)}, f32[13,1024]{1,0:T(8,128)S(1)}, f32[13,16384]{1,0:T(8,128)S(1)}, s32[16384]{0:T(1024)S(1)}, s32[]{:T(128)}, /*index=5*/s32[]{:T(128)}, s32[]{:T(128)}, s32[]{:T(128)}) while((s32[]{:T(128)}, f32[13,1024]{1,0:T(8,128)S(1)}, f32[13,16384]{1,0:T(8,128)S(1)}, s32[16384]{0:T(1024)S(1)}, s32[]{:T(128)}, ...), condition=%wide.region_15.0_spmd.clone, body=%wide.region_14.0_spmd.clone.sunk | while | flops 329279488 | bytes 274581 | solution.py:32
  678.3 15.5 %reshape.1706 = f32[16384,1,13]{2,1,0:T(1,128)} reshape(f32[128,1664]{1,0:T(8,128)} %reduce.1031) | data formatting | bytes 1703936
  693.8 16.7 %copy.231 = f32[1,13,16384]{2,0,1:T(1,128)} copy(f32[1,13,16384]{1,0,2:T(1,128)} %bitcast.1225) | data formatting | bytes 1703936 | tf_op jit(solution)/shard_map/all_to_all | solution.py:57
  731.9 26.8 %while.114 = (s32[]{:T(128)}, f32[13,16384]{1,0:T(8,128)}, s32[16384]{0:T(1024)S(1)}, f32[13,1024]{1,0:T(8,128)S(1)}, s32[]{:T(128)}, /*index=5*/s32[]{:T(128)}, s32[]{:T(128)}, s32[]{:T(128)}) while((s32[]{:T(128)}, f32[13,16384]{1,0:T(8,128)}, s32[16384]{0:T(1024)S(1)}, f32[13,1024]{1,0:T(8,128)S(1)}, s32[]{:T(128)}, ...), condition=%wide.region_17.0_spmd.clone, body=%wide.region_16.0_spmd.clone.sunk | while | flops 329252864 | bytes 209035 | solution.py:52
  764.1 67.3 %psum.45 = f32[]{:T(128)} all-reduce(f32[]{:T(128)} %multiply_reduce_fusion.2), channel_id=1, replica_groups=mesh['store'=8,'sku'=16] {'store','sku'}, use_global_device_ids=true, to_apply=%region_19.0 | all-reduce | flops 1 | bytes 8 | tf_op jit(solution)/shard_map/psum | solution.py:116
  836.8 62.7 %psum.46 = f32[]{:T(128)} all-reduce(f32[]{:T(128)} %get-tuple-element.1462), channel_id=1, replica_groups=mesh['store'=8,'sku'=16] {'store','sku'}, use_global_device_ids=true, to_apply=%region_21.0 | all-reduce | flops 1 | bytes 8 | tf_op jit(solution)/shard_map/psum | solution.py:74
  903.0 15.6 %copy.238 = f32[1,13,16384]{1,0,2:T(1,128)} copy(f32[1,13,16384]{2,1,0:T(8,128)} %multiply_add_fusion) | data formatting | bytes 1703936 | tf_op jit(solution)/shard_map/add | solution.py:120
  918.6 74.4 %reduce.1032 = f32[16384,13]{1,0:T(8,128)} reduce(f32[16384,1,13]{2,1,0:T(1,128)} %bitcast.1221, f32[]{:T(128)} %broadcast.564), dimensions={1}, to_apply=%bitcast.1183.reduce_sub_computation | reduce | bytes 1703940
  1008.3 29.3 %while.119 = (s32[]{:T(128)}, f32[13,1024]{1,0:T(8,128)S(1)}, f32[13,16384]{1,0:T(8,128)}, s32[16384]{0:T(1024)S(1)}, s32[]{:T(128)}, /*index=5*/s32[]{:T(128)}, s32[]{:T(128)}, s32[]{:T(128)}) while((s32[]{:T(128)}, f32[13,1024]{1,0:T(8,128)S(1)}, f32[13,16384]{1,0:T(8,128)}, s32[16384]{0:T(1024)S(1)}, s32[]{:T(128)}, ...), condition=%wide.region_23.0_spmd.clone, body=%wide.region_22.0_spmd.clone.sunk | while | flops 329279488 | bytes 262293 | solution.py:32
  1042.3 15.5 %reshape.1708 = f32[16384,1,13]{2,1,0:T(1,128)} reshape(f32[128,1664]{1,0:T(8,128)} %reduce.1033) | data formatting | bytes 1703936
  1057.8 16.5 %copy.239 = f32[1,13,16384]{2,0,1:T(1,128)} copy(f32[1,13,16384]{1,0,2:T(1,128)} %bitcast.1226) | data formatting | bytes 1703936 | tf_op jit(solution)/shard_map/all_to_all | solution.py:57
  1095.8 26.8 %while.115 = (s32[]{:T(128)}, f32[13,16384]{1,0:T(8,128)}, s32[16384]{0:T(1024)S(1)}, f32[13,1024]{1,0:T(8,128)S(1)}, s32[]{:T(128)}, /*index=5*/s32[]{:T(128)}, s32[]{:T(128)}, s32[]{:T(128)}) while((s32[]{:T(128)}, f32[13,16384]{1,0:T(8,128)}, s32[16384]{0:T(1024)S(1)}, f32[13,1024]{1,0:T(8,128)S(1)}, s32[]{:T(128)}, ...), condition=%wide.region_25.0_spmd.clone, body=%wide.region_24.0_spmd.clone.sunk | while | flops 329252864 | bytes 209035 | solution.py:52
  1128.3 67.5 %psum.47 = f32[]{:T(128)} all-reduce(f32[]{:T(128)} %multiply_reduce_fusion), channel_id=1, replica_groups=mesh['store'=8,'sku'=16] {'store','sku'}, use_global_device_ids=true, to_apply=%region_27.0 | all-reduce | flops 1 | bytes 8 | tf_op jit(solution)/shard_map/psum | solution.py:116
  (772 shorter events, 456.2 us)
Async XLA Ops:
  91.0 21.0 %copy-start.4 = (f32[1,13,16384]{2,0,1:T(1,128)S(1)}, f32[1,13,16384]{2,0,1:T(1,128)}, u32[]{:S(2)}) copy-start(f32[1,13,16384]{2,0,1:T(1,128)} %param.24) | copy-start | bytes 2555908
  91.0 21.5 %copy-start.6 = (s32[16384]{0:T(1024)S(1)}, s32[16384]{0:T(1024)}, u32[]{:S(2)}) copy-start(s32[16384]{0:T(1024)} %param.30) | copy-start | bytes 196612
  100.0 34.6 %copy-start.7 = (f32[1,13,1024]{2,0,1:T(1,128)S(1)}, f32[1,13,1024]{2,0,1:T(1,128)}, u32[]{:S(2)}) copy-start(f32[1,13,1024]{2,0,1:T(1,128)} %param.27) | copy-start | bytes 159748
  100.0 34.6 %copy-start.9 = (f32[1,13,1024]{2,0,1:T(1,128)S(1)}, f32[1,13,1024]{2,0,1:T(1,128)}, u32[]{:S(2)}) copy-start(f32[1,13,1024]{2,0,1:T(1,128)} %param.26) | copy-start | bytes 159748
  100.0 34.6 %all-to-all-start = ((f32[128,1,1664]{2,1,0:T(1,128)}), f32[128,1,1664]{2,1,0:T(1,128)S(1)}, u32[]{:S(2)}, u32[]{:S(2)}) async-start(f32[128,1,1664]{2,1,0:T(1,128)} %reshape.1701), calls=%async_computation | async-start | bytes 1703936 | tf_op jit(solution)/shard_map/all_to_all | solution.py:57
  137.3 30.6 %copy-start.5 = (f32[32,13,128]{2,0,1:T(8,128)S(1)}, f32[32,13,128]{2,0,1:T(8,128)}, u32[]{:S(2)}) copy-start(f32[32,13,128]{2,0,1:T(8,128)} %param.29) | copy-start | bytes 638980
  137.3 30.6 %copy-start.8 = (f32[32,13,128]{2,0,1:T(8,128)S(1)}, f32[32,13,128]{2,0,1:T(8,128)}, u32[]{:S(2)}) copy-start(f32[32,13,128]{2,0,1:T(8,128)} %param.28) | copy-start | bytes 638980
  137.3 30.6 %copy-start.10 = (s32[128]{0:T(128)S(1)}, s32[128]{0:T(128)}, u32[]{:S(2)}) copy-start(s32[128]{0:T(128)} %param.31) | copy-start | bytes 1540
  174.5 31.9 %all-to-all-start.1 = ((f32[128,1,13,128]{3,1,2,0:T(1,128)}), f32[128,1,13,128]{3,1,2,0:T(1,128)S(1)}, u32[]{:S(2)}, u32[]{:S(2)}) async-start(f32[128,1,13,128]{3,1,2,0:T(1,128)} %copy.217), calls=%async_computation.1 | async-start | bytes 1703936 | tf_op jit(solution)/shard_map/all_to_all | solution.py:62
  303.6 32.2 %all-to-all-start.2 = ((f32[128,1,1664]{2,1,0:T(1,128)}), f32[128,1,1664]{2,1,0:T(1,128)S(1)}, u32[]{:S(2)}, u32[]{:S(2)}) async-start(f32[128,1,1664]{2,1,0:T(1,128)} %reshape.1703), calls=%async_computation.2 | async-start | bytes 1703936 | tf_op jit(solution)/shard_map/all_to_all | solution.py:57
  375.5 32.0 %all-to-all-start.3 = ((f32[128,1,13,128]{3,1,2,0:T(1,128)}), f32[128,1,13,128]{3,1,2,0:T(1,128)}, u32[]{:S(2)}, u32[]{:S(2)}) async-start(f32[128,1,13,128]{3,1,2,0:T(1,128)} %copy.225), calls=%async_computation.3 | async-start | bytes 1703936 | tf_op jit(solution)/shard_map/all_to_all | solution.py:62
  385.7 24.1 %copy-start = (f32[1,13,16384]{2,0,1:T(1,128)S(1)}, f32[1,13,16384]{2,0,1:T(1,128)}, u32[]{:S(2)}) copy-start(f32[1,13,16384]{2,0,1:T(1,128)} %param.25) | copy-start | bytes 2555908
  407.5 1.7 copy-start.2
  645.1 28.5 %all-to-all-start.4 = ((f32[128,1,1664]{2,1,0:T(1,128)}), f32[128,1,1664]{2,1,0:T(1,128)}, u32[]{:S(2)}, u32[]{:S(2)}) async-start(f32[128,1,1664]{2,1,0:T(1,128)} %reshape.1705), calls=%async_computation.4 | async-start | bytes 1703936 | tf_op jit(solution)/shard_map/all_to_all | solution.py:57
  720.6 38.1 %all-to-all-start.5 = ((f32[128,1,13,128]{3,1,2,0:T(1,128)}), f32[128,1,13,128]{3,1,2,0:T(1,128)}, u32[]{:S(2)}, u32[]{:S(2)}) async-start(f32[128,1,13,128]{3,1,2,0:T(1,128)} %copy.234), calls=%async_computation.5 | async-start | bytes 1703936 | tf_op jit(solution)/shard_map/all_to_all | solution.py:62
  760.7 1.0 copy-start.1
  1002.0 35.7 %all-to-all-start.6 = ((f32[128,1,1664]{2,1,0:T(1,128)}), f32[128,1,1664]{2,1,0:T(1,128)}, u32[]{:S(2)}, u32[]{:S(2)}) async-start(f32[128,1,1664]{2,1,0:T(1,128)} %reshape.1707), calls=%async_computation.6 | async-start | bytes 1703936 | tf_op jit(solution)/shard_map/all_to_all | solution.py:57
  1084.5 38.1 %all-to-all-start.7 = ((f32[128,1,13,128]{3,1,2,0:T(1,128)}), f32[128,1,13,128]{3,1,2,0:T(1,128)}, u32[]{:S(2)}, u32[]{:S(2)}) async-start(f32[128,1,13,128]{3,1,2,0:T(1,128)} %copy.242), calls=%async_computation.7 | async-start | bytes 1703936 | tf_op jit(solution)/shard_map/all_to_all | solution.py:62
  1124.6 1.0 copy-start.3
